TPU v7x, 32 devices: a whole 2x2x4 slice. The times are simulated.
32 devices in a mesh: term: 4 (over x, core), sec: 8 (over z, y).
Axes of the slice: x: 2, y: 2, z: 4, core: 2. Of those that a mesh axis runs over, the one named last changes fastest.
Arguments:
- psi_tiles: bfloat16 [192, 512, 512], P('sec'), may hold values from -6 to 6
- sectors: int32 [192, 2], P('sec'), may hold values from 0 to 15
- sources: int32 [4, 192], P('term', 'sec'), may hold values from 0 to 191, as said below
- left_env: bfloat16 [4, 16, 512, 512], P('term', None, 'sec'), may hold values from -0.25 to 0.25
- right_env: bfloat16 [4, 16, 512, 512], P('term', None, 'sec'), may hold values from -0.25 to 0.25
Outputs:
- applied: bfloat16 [192, 512, 512], P('sec', 'term')
Inputs may be any that keep to these rules, and one draw needn't show every extreme that they name: sources[t, k] lies in the same aligned block of 24 tiles as k, and each row maps each such block one to one onto itself.
All inputs are finite; a program needn't handle non-finite values.
Results may differ from a plain program's by a relative error of at most 0.013.
Values may be sent and summed in bfloat16 or wider, within the bound.
A program may use at most 192 MiB of HBM per device.

v0:
```python
import jax
import jax.numpy as jnp
from jax import lax
from jax.sharding import PartitionSpec as P


def body(psi_tiles, sectors, sources, left_env, right_env):
    tile_count = psi_tiles.shape[0]
    width = psi_tiles.shape[2]
    local_ids = sources[0] - lax.axis_index("sec") * tile_count
    moved = jnp.take(psi_tiles, local_ids, axis=0)
    left_ids = sectors[:, 0]
    right_ids = sectors[:, 1]
    chosen = jnp.take(lax.all_gather(right_env[0], "sec", axis=1, tiled=True), right_ids, axis=0)
    half = jnp.einsum("kij,kjl->kil", moved, chosen, preferred_element_type=jnp.float32).astype(
        jnp.bfloat16
    )
    chosen = jnp.take(lax.all_gather(left_env[0], "sec", axis=1, tiled=True), left_ids, axis=0)
    term_out = jnp.einsum("kij,kjl->kil", chosen, half, preferred_element_type=jnp.float32)
    share_rows = width // lax.axis_size("term")
    summed = lax.psum(term_out.astype(jnp.bfloat16), "term").astype(jnp.float32)
    kept = lax.dynamic_slice_in_dim(summed, lax.axis_index("term") * share_rows, share_rows, 1)
    return kept.astype(jnp.bfloat16)


def solution(mesh):
    placed = (
        P("sec", None, None),
        P("sec", None),
        P("term", "sec"),
        P("term", None, "sec", None),
        P("term", None, "sec", None),
    )
    return jax.shard_map(
        body, mesh=mesh, in_specs=placed, out_specs=P("sec", "term", None), check_vma=False
    )
```

profile of v0, /device:TPU:24, one launch (start us, length us, event | category | flops | bytes accessed | tf_op | source)
XLA Modules:
  0.0 521.4 jit_solution(4333195429410289750)
XLA Ops:
  6.5 0.0 all-gather.7.cloned.1.call-start
  6.5 0.7 all-gather.7.cloned.1.call-update
  7.3 0.0 all-gather.5.cloned.1.call-start
  7.3 0.7 all-gather.5.cloned.1.call-update
  8.0 0.0 all-reduce.2.cloned.1.call-start
  8.1 0.7 fusion.30
  8.7 0.0 copy-start
  8.7 0.0 copy-start.1
  8.7 10.8 %gather_fusion = bf16[24,512,512]{2,1,0:T(8,128)(2,1)} fusion(bf16[24,512,512]{2,1,0:T(8,128)(2,1)} %param.7, s32[1024]{0:T(1024)S(1)} %pad_clamp_fusion.1), kind=kCustom, calls=%fused_computation.2 | custom fusion | bytes 25165920 | tf_op jit(solution)/shard_map/jit(_take)/gather | solution.py:11
  19.5 0.0 copy-done
  19.5 0.0 copy-done.1
  19.6 114.0 %all-gather.7.cloned.1.call-done = bf16[1,16,512,512]{3,2,1,0:T(8,128)(2,1)} async-done(((bf16[1,16,64,512]{3,2,1,0:T(8,128)(2,1)}), bf16[1,16,512,512]{3,2,1,0:T(8,128)(2,1)}) %all-gather.7.cloned.1.call-update) | async-done | bytes 8388624 | tf_op jit(solution)/shard_map/all_gather | solution.py:14
  133.5 9.5 %gather_fusion.2 = bf16[24,512,512]{2,1,0:T(8,128)(2,1)} fusion(bf16[16,512,512]{2,1,0:T(8,128)(2,1)} %bitcast.14, s32[1024]{0:T(1024)S(1)} %get-tuple-element.12), kind=kCustom, calls=%fused_computation.1.clone | custom fusion | bytes 25165920 | tf_op jit(solution)/shard_map/jit(_take)/gather | solution.py:14
  143.0 115.8 %all-gather.5.cloned.1.call-done = bf16[1,16,512,512]{3,2,1,0:T(8,128)(2,1)} async-done(((bf16[1,16,64,512]{3,2,1,0:T(8,128)(2,1)}), bf16[1,16,512,512]{3,2,1,0:T(8,128)(2,1)}) %all-gather.5.cloned.1.call-update) | async-done | bytes 8388624 | tf_op jit(solution)/shard_map/all_gather | solution.py:18
  258.9 9.5 %gather_fusion.1 = bf16[24,512,512]{2,1,0:T(8,128)(2,1)} fusion(bf16[16,512,512]{2,1,0:T(8,128)(2,1)} %bitcast.15, s32[1024]{0:T(1024)S(1)} %get-tuple-element.13), kind=kCustom, calls=%fused_computation.clone | custom fusion | bytes 25165920 | tf_op jit(solution)/shard_map/jit(_take)/gather | solution.py:18
  268.4 21.7 %fusion.19 = bf16[24,512,512]{2,1,0:T(8,128)(2,1)} fusion(bf16[24,512,512]{2,1,0:T(8,128)(2,1)} %gather_fusion.2, bf16[24,512,512]{2,1,0:T(8,128)(2,1)} %gather_fusion, pred[24]{0:T(512)(128)(4,1)S(1)} %get-tuple-element.10, pred[24]{0:T(512)(128)(4,1)S(1)} %compare_and_fusion.2, bf16[24,512,512]{2,1,0:T(8,128)(2,1)} %gather_fusion.1, ...), kind=kOutput, calls=%fused_computation.12 | convolution fusion | flops 12916359168 | bytes 50331720 | tf_op jit(solution)/shard_map/kij,kjl->kil/dot_general | solution.py:19
  290.1 0.0 all-reduce.2.cloned.1.call-update
  290.1 220.9 %all-reduce.2.cloned.1.call-done = bf16[24,512,512]{2,1,0:T(8,128)(2,1)} async-done(((bf16[24,512,512]{2,1,0:T(8,128)(2,1)}), bf16[24,512,512]{2,1,0:T(8,128)(2,1)}) %all-reduce.2.cloned.1.call-update) | async-done | bytes 12582928 | tf_op jit(solution)/shard_map/psum | solution.py:21
  511.0 3.9 convert_convert_fusion
  (4 shorter events, 0.0 us)
Async XLA Ops:
  6.5 127.0 %all-gather.7.cloned.1.call-start = ((), (), s32[]{:S(2)}) async-start(), calls=%async_computation.2 | async-start | bytes 9437184 | tf_op jit(solution)/shard_map/all_gather | solution.py:14
  7.3 251.6 %all-gather.5.cloned.1.call-start = ((), (), s32[]{:S(2)}) async-start(), calls=%async_computation.1 | async-start | bytes 9437184 | tf_op jit(solution)/shard_map/all_gather | solution.py:18
  8.0 503.0 %all-reduce.2.cloned.1.call-start = ((), (), s32[]{:S(2)}) async-start(), calls=%async_computation | async-start | bytes 25165824 | tf_op jit(solution)/shard_map/psum | solution.py:21
  8.7 10.8 %copy-start = (s32[24,2]{0,1:T(2,128)S(1)}, s32[24,2]{0,1:T(2,128)}, u32[]{:S(2)}) copy-start(s32[24,2]{0,1:T(2,128)} %param.8) | copy-start | bytes 580
  8.7 10.8 %copy-start.1 = (s32[1,24]{1,0:T(1,128)S(1)}, s32[1,24]{1,0:T(1,128)}, u32[]{:S(2)}) copy-start(s32[1,24]{1,0:T(1,128)} %param.9) | copy-start | bytes 292
Sparse Core Ops, SparseCore 0:
  9.5 123.9 all-gather.6
  135.7 123.0 all-gather.4
  290.2 220.7 all-reduce.1
where the time goes:
time: 523 us; the launch traced here: 521 us
  waiting for transfers between devices  452 us (86%)
  local copies, waits for them, and re-layouts  29.8 us (6%)
  matrix products  21.7 us (4%)
  between operations  13.2 us (3%)
    psum x1, waiting for transfers between devices, body(): summed = lax.psum(term_out.astype(jnp.bfloat16), 'term').astype(jnp.float32)  221 us
    all_gather x1, waiting for transfers between devices, body(): lax.all_gather(left_env[0], 'sec', axis=1, tiled=True)  116 us
    all_gather x1, waiting for transfers between devices, body(): lax.all_gather(right_env[0], 'sec', axis=1, tiled=True)  114 us
    dot_general x1, matrix products, body(): jnp.einsum('kij,kjl->kil', chosen, half, preferred_element_type=jnp.float32)  21.7 us
    gather x1, local copies, waits for them, and re-layouts, body(): moved = jnp.take(psi_tiles, local_ids, axis=0)  10.8 us
  transfers between devices with their start and end apart: 3, of which 3 were waited for; matrix products, arithmetic and copies ran while one was open for 4% of the time, Pallas kernels for 0%

commit v1 on v0

v1 whole, which is shorter than its diff:
```python
import functools

import jax
import jax.numpy as jnp
from jax import lax
from jax.experimental import pallas as pl
from jax.experimental.pallas import tpu as pltpu
from jax.sharding import PartitionSpec as P

MESH = pl.DeviceIdType.MESH
GROUPS = 4


def kernel(
    n,
    terms,
    sectors,
    sources,
    psi_h,
    left_h,
    right_h,
    out_h,
    psi_v,
    right_v,
    left_v,
    left_now,
    half_v,
    core_in,
    chip_in,
    local_sem,
    recv_sem,
    pair_sem,
    up_sem,
    down_sem,
    core_send,
    core_recv,
    chip_send,
    chip_recv,
    out_sem,
):
    tiles = psi_h.shape[0]
    rows = right_h.shape[1]
    line = n // 2
    wide = 2 * rows
    per_owner = line // terms
    size = tiles // GROUPS
    term = lax.axis_index("term")
    sec = lax.axis_index("sec")
    core = lax.rem(term, 2)
    chip = term // 2
    spot = sec // 2
    side = lax.rem(sec, 2)
    pair = spot * 2 + 1 - side
    other_core = chip * 2 + 1 - core
    other_chip = (1 - chip) * 2 + core
    has_up = spot + 1 < line
    has_down = spot > 0
    gathered = (right_v, left_v)
    owned = (right_h, left_h)

    def slot_of(place, parity):
        return place * 2 + parity

    def window(kind, slot):
        return gathered[kind].at[:, pl.ds(pl.multiple_of(slot * rows, rows), rows), :]

    def env_copy(kind, slot, src, target, sem):
        return pltpu.make_async_remote_copy(
            src_ref=src,
            dst_ref=window(kind, slot),
            send_sem=sem,
            recv_sem=recv_sem.at[kind, slot],
            device_id={"sec": target},
            device_id_type=MESH,
        )

    def to_pair(kind, place, src):
        return env_copy(kind, slot_of(place, side), src, pair, pair_sem.at[kind, place])

    def to_up(kind, place, src):
        return env_copy(kind, slot_of(place, side), src, sec + 2, up_sem.at[kind, place])

    def to_down(kind, place, src):
        return env_copy(kind, slot_of(place, side), src, sec - 2, down_sem.at[kind, place])

    def await_slot(kind, slot):
        env_copy(kind, slot, owned[kind], pair, pair_sem.at[kind, 0]).wait_recv()

    def push_own(kind):
        @pl.when(has_down)
        def _():
            to_down(kind, spot, owned[kind]).start()

        @pl.when(has_up)
        def _():
            to_up(kind, spot, owned[kind]).start()

        to_pair(kind, spot, owned[kind]).start()

    def forward(kind, step):
        @pl.when(spot - step >= 0)
        def _():
            place = spot - step
            slot = slot_of(place, side)
            await_slot(kind, slot)

            @pl.when(has_up)
            def _():
                to_up(kind, place, window(kind, slot)).start()

            to_pair(kind, place, window(kind, slot)).start()

        @pl.when(spot + step < line)
        def _():
            place = spot + step
            slot = slot_of(place, side)
            await_slot(kind, slot)

            @pl.when(has_down)
            def _():
                to_down(kind, place, window(kind, slot)).start()

            to_pair(kind, place, window(kind, slot)).start()

    def block_rows(block):
        return pl.ds(pl.multiple_of(block * wide, wide), wide)

    def group_rows(group):
        return pl.ds(group * size, size)

    def core_copy(block, group):
        owner = block // per_owner
        slot = (owner // 2) * per_owner + lax.rem(block, per_owner)
        return pltpu.make_async_remote_copy(
            src_ref=psi_v.at[group_rows(group), block_rows(block), :],
            dst_ref=core_in.at[slot, group_rows(group)],
            send_sem=core_send.at[block, group],
            recv_sem=core_recv.at[block, group],
            device_id={"term": other_core},
            device_id_type=MESH,
        )

    def chip_copy(block, group):
        return pltpu.make_async_remote_copy(
            src_ref=psi_v.at[group_rows(group), block_rows(block), :],
            dst_ref=chip_in.at[lax.rem(block, per_owner), group_rows(group)],
            send_sem=chip_send.at[block, group],
            recv_sem=chip_recv.at[block, group],
            device_id={"term": other_chip},
            device_id_type=MESH,
        )

    barrier = pltpu.get_barrier_semaphore()
    pl.semaphore_signal(barrier, inc=1, device_id={"sec": pair}, device_id_type=MESH)
    pl.semaphore_signal(barrier, inc=1, device_id={"term": other_core}, device_id_type=MESH)
    pl.semaphore_signal(barrier, inc=1, device_id={"term": other_chip}, device_id_type=MESH)

    @pl.when(has_up)
    def _():
        pl.semaphore_signal(barrier, inc=1, device_id={"sec": sec + 2}, device_id_type=MESH)

    @pl.when(has_down)
    def _():
        pl.semaphore_signal(barrier, inc=1, device_id={"sec": sec - 2}, device_id_type=MESH)

    pl.semaphore_wait(barrier, 3 + has_up.astype(jnp.int32) + has_down.astype(jnp.int32))

    push_own(0)
    locals_ = (
        pltpu.make_async_copy(psi_h, psi_v, local_sem.at[0]),
        pltpu.make_async_copy(right_h, window(0, sec), local_sem.at[1]),
        pltpu.make_async_copy(left_h, window(1, sec), local_sem.at[2]),
    )
    for copy in locals_:
        copy.start()

    @pl.loop(1, line)
    def _(step):
        forward(0, step)

    push_own(1)
    for copy in locals_:
        copy.wait()

    @pl.loop(0, line)
    def _(place):
        await_slot(0, slot_of(place, 1 - side))

    forward(1, 1)

    @pl.loop(0, tiles)
    def _(k):
        moved = psi_v[lax.rem(sources[0, k], tiles)]
        chosen = right_v[sectors[k, 1]]
        half_v[k] = jnp.dot(moved, chosen, preferred_element_type=jnp.float32).astype(jnp.bfloat16)

    def apply_left(block):
        owner = block // per_owner
        owner_core = lax.rem(owner, 2)
        owner_chip = owner // 2
        await_slot(1, slot_of(block, 1 - side))

        @pl.loop(0, left_v.shape[0])
        def _(i):
            left_now[i] = left_v[i, block_rows(block), :]

        @pl.loop(0, GROUPS)
        def _(group):
            @pl.loop(0, size // 2)
            def _(i):
                for j in range(2):
                    k = group * size + i * 2 + j
                    chosen = left_now[sectors[k, 0]]
                    psi_v[k, block_rows(block), :] = jnp.dot(
                        chosen, half_v[k], preferred_element_type=jnp.float32
                    ).astype(jnp.bfloat16)

            @pl.when(core != owner_core)
            def _():
                core_copy(block, group).start()

        @pl.when((core == owner_core) & (chip != owner_chip))
        def _():
            slot = owner_chip * per_owner + lax.rem(block, per_owner)

            @pl.loop(0, GROUPS)
            def _(group):
                core_copy(block, group).wait_recv()

                @pl.loop(0, size)
                def _(i):
                    k = group * size + i
                    psi_v[k, block_rows(block), :] = (
                        psi_v[k, block_rows(block), :].astype(jnp.float32)
                        + core_in[slot, k].astype(jnp.float32)
                    ).astype(jnp.bfloat16)

                chip_copy(block, group).start()

    @pl.loop(0, line)
    def _(step):
        @pl.when(step > 1)
        def _():
            forward(1, step)

        @pl.when(spot - step >= 0)
        def _():
            apply_left(spot - step)

        @pl.when((step > 0) & (spot + step < line))
        def _():
            apply_left(spot + step)

    def out_copy(j, group):
        block = term * per_owner + j
        return pltpu.make_async_copy(
            psi_v.at[group_rows(group), block_rows(block), :],
            out_h.at[group_rows(group), pl.ds(pl.multiple_of(j * wide, wide), wide), :],
            out_sem.at[j, group],
        )

    @pl.loop(0, per_owner)
    def _(j):
        block = term * per_owner + j

        @pl.loop(0, GROUPS)
        def _(group):
            core_copy(block, group).wait_recv()
            chip_copy(block, group).wait_recv()

            @pl.loop(0, size)
            def _(i):
                k = group * size + i
                psi_v[k, block_rows(block), :] = (
                    psi_v[k, block_rows(block), :].astype(jnp.float32)
                    + core_in[chip * per_owner + j, k].astype(jnp.float32)
                    + chip_in[j, k].astype(jnp.float32)
                ).astype(jnp.bfloat16)

            out_copy(j, group).start()

    @pl.loop(0, line)
    def _(place):
        for kind in range(2):
            to_pair(kind, place, owned[kind]).wait_send()

            @pl.when(has_up & (place <= spot))
            def _():
                to_up(kind, place, owned[kind]).wait_send()

            @pl.when(has_down & (place >= spot))
            def _():
                to_down(kind, place, owned[kind]).wait_send()

        owner = place // per_owner

        @pl.loop(0, GROUPS)
        def _(group):
            @pl.when(core != lax.rem(owner, 2))
            def _():
                core_copy(place, group).wait_send()

            @pl.when((core == lax.rem(owner, 2)) & (chip != owner // 2))
            def _():
                chip_copy(place, group).wait_send()

    @pl.loop(0, per_owner)
    def _(j):
        @pl.loop(0, GROUPS)
        def _(group):
            out_copy(j, group).wait()


def body(psi_tiles, sectors, sources, left_env, right_env):
    n = lax.axis_size("sec")
    terms = lax.axis_size("term")
    tiles, width, _ = psi_tiles.shape
    nsec = left_env.shape[1]
    line = n // 2
    wide = 2 * width // n
    kind = jnp.bfloat16
    dma = pltpu.SemaphoreType.DMA
    return pl.pallas_call(
        functools.partial(kernel, n, terms),
        out_shape=jax.ShapeDtypeStruct((tiles, width // terms, width), kind),
        in_specs=[pl.BlockSpec(memory_space=pltpu.SMEM)] * 2 + [pl.BlockSpec(memory_space=pl.ANY)] * 3,
        out_specs=pl.BlockSpec(memory_space=pl.ANY),
        scratch_shapes=[
            pltpu.VMEM((tiles, width, width), kind),
            pltpu.VMEM((nsec, width, width), kind),
            pltpu.VMEM((nsec, width, width), kind),
            pltpu.VMEM((nsec, wide, width), kind),
            pltpu.VMEM((tiles, width, width), kind),
            pltpu.VMEM((line // 2, tiles, wide, width), kind),
            pltpu.VMEM((line // terms, tiles, wide, width), kind),
            dma((3,)),
            dma((2, n)),
            dma((2, line)),
            dma((2, line)),
            dma((2, line)),
            dma((line, GROUPS)),
            dma((line, GROUPS)),
            dma((line, GROUPS)),
            dma((line, GROUPS)),
            dma((line // terms, GROUPS)),
        ],
        compiler_params=pltpu.CompilerParams(
            collective_id=0, has_side_effects=True, vmem_limit_bytes=60 * 1024 * 1024
        ),
        cost_estimate=pl.CostEstimate(
            flops=4 * tiles * width**3,
            bytes_accessed=2 * (tiles * width * width + 2 * nsec * width * width),
            transcendentals=0,
        ),
    )(sectors, sources, psi_tiles, left_env[0], right_env[0])


def solution(mesh):
    placed = (
        P("sec", None, None),
        P("sec", None),
        P("term", "sec"),
        P("term", None, "sec", None),
        P("term", None, "sec", None),
    )
    return jax.shard_map(
        body, mesh=mesh, in_specs=placed, out_specs=P("sec", "term", None), check_vma=False
    )
```

time: 523 us -> 258 us (0.49)
  waiting for transfers between devices: 452 us -> 0 us
  Pallas kernels: 0 us -> 253 us
  local copies, waits for them, and re-layouts: 29.8 us -> 5.21 us
  matrix products: 21.7 us -> 0 us
  between operations: 13.2 us -> 0.01 us
    pallas_call x0 -> x1, Pallas kernels: none -> 253 us  [body(): pl.pallas_call(functools.partial(kernel, n, terms), out_shape=jax.ShapeDt...]
    all_gather x2 -> x0, waiting for transfers between devices: 230 us -> none  [the longest x1 116 us: body(): lax.all_gather(left_env[0], 'sec', axis=1, tiled=True)]
    psum x1 -> x0, waiting for transfers between devices: 221 us -> none  [body(): summed = lax.psum(term_out.astype(jnp.bfloat16), 'term').astype(jnp.float32)]
    gather x3 -> x0, local copies, waits for them, and re-layouts: 29.8 us -> none  [the longest x1 10.8 us: body(): moved = jnp.take(psi_tiles, local_ids, axis=0)]
    dot_general x1 -> x0, matrix products: 21.7 us -> none  [body(): jnp.einsum('kij,kjl->kil', chosen, half, preferred_element_type=jnp.float32)]
  transfers between devices with their start and end apart: 3 -> 0, of which waited for: 3 -> 0; matrix products, arithmetic and copies ran while one was open for 4% -> 0% of each run, Pallas kernels for 0% -> 0%
where the time goes in v1:
time: 258 us
  Pallas kernels  253 us (98%)
  local copies, waits for them, and re-layouts  5.21 us (2%)
    pallas_call x1, Pallas kernels, body(): pl.pallas_call(functools.partial(kernel, n, terms), out_shape=jax.ShapeDt...  253 us
    unnamed x2, local copies, waits for them, and re-layouts  5.21 us

profile of v1, /device:TPU:24, one launch (start us, length us, event | category | flops | bytes accessed | tf_op | source)
XLA Modules:
  0.0 258.1 jit_solution(14413642077205341881)
XLA Ops:
  0.0 1.4 copy.6.sectors
  1.4 252.9 %shard_map.55 = bf16[24,128,512]{2,1,0:T(8,128)(2,1)} custom-call(s32[24,2]{1,0:T(8,128)} %copy.6.sectors, s32[1,24]{1,0:T(1,128)} %sources.1, bf16[24,512,512]{2,1,0:T(8,128)(2,1)} %psi_h.1, bf16[16,64,512]{2,1,0:T(8,128)(2,1)} %bitcast.2, bf16[16,64,512]{2,1,0:T(8,128)(2,1)} %bitcast.3), custom_call_target="tpu_custom_call" | custom-call | flops 12884901888 | bytes 29360128 | tf_op jit(solution)/shard_map/pallas_call | solution.py:323
  254.3 3.9 %copy.8 = bf16[24,128,512]{2,1,0:T(8,128)(2,1)} copy(bf16[24,128,512]{2,1,0:T(8,128)(2,1)} %shard_map.55) | data formatting | bytes 6291456

commit v2 on v1

--- a/solution.py
+++ b/solution.py
@@ -32,6 +32,7 @@
     pair_sem,
     up_sem,
     down_sem,
+    mate_sem,
     core_send,
     core_recv,
     chip_send,
@@ -55,6 +56,7 @@
     other_chip = (1 - chip) * 2 + core
     has_up = spot + 1 < line
     has_down = spot > 0
+    mate = spot + 1 - 2 * lax.rem(spot, 2)
     gathered = (right_v, left_v)
     owned = (right_h, left_h)
 
@@ -83,6 +85,10 @@
     def to_down(kind, place, src):
         return env_copy(kind, slot_of(place, side), src, sec - 2, down_sem.at[kind, place])
 
+    def to_mate(kind):
+        slot = slot_of(spot, 1 - side)
+        return env_copy(kind, slot, window(kind, slot), mate * 2 + side, mate_sem.at[kind])
+
     def await_slot(kind, slot):
         env_copy(kind, slot, owned[kind], pair, pair_sem.at[kind, 0]).wait_recv()
 
@@ -96,6 +102,15 @@
             to_up(kind, spot, owned[kind]).start()
 
         to_pair(kind, spot, owned[kind]).start()
+
+    def send_pair(kind, place, slot):
+        if kind == 0:
+            to_pair(kind, place, window(kind, slot)).start()
+        else:
+
+            @pl.when(place != mate)
+            def _():
+                to_pair(kind, place, window(kind, slot)).start()
 
     def forward(kind, step):
         @pl.when(spot - step >= 0)
@@ -108,7 +123,7 @@
             def _():
                 to_up(kind, place, window(kind, slot)).start()
 
-            to_pair(kind, place, window(kind, slot)).start()
+            send_pair(kind, place, slot)
 
         @pl.when(spot + step < line)
         def _():
@@ -120,7 +135,7 @@
             def _():
                 to_down(kind, place, window(kind, slot)).start()
 
-            to_pair(kind, place, window(kind, slot)).start()
+            send_pair(kind, place, slot)
 
     def block_rows(block):
         return pl.ds(pl.multiple_of(block * wide, wide), wide)
@@ -200,6 +215,10 @@
         owner_chip = owner // 2
         await_slot(1, slot_of(block, 1 - side))
 
+        @pl.when(block == spot)
+        def _():
+            to_mate(1).start()
+
         @pl.loop(0, left_v.shape[0])
         def _(i):
             left_now[i] = left_v[i, block_rows(block), :]
@@ -279,10 +298,17 @@
 
             out_copy(j, group).start()
 
+    to_mate(1).wait_send()
+
     @pl.loop(0, line)
     def _(place):
+        to_pair(0, place, owned[0]).wait_send()
+
+        @pl.when(place != mate)
+        def _():
+            to_pair(1, place, owned[1]).wait_send()
+
         for kind in range(2):
-            to_pair(kind, place, owned[kind]).wait_send()
 
             @pl.when(has_up & (place <= spot))
             def _():
@@ -338,6 +364,7 @@
             dma((2, line)),
             dma((2, line)),
             dma((2, line)),
+            dma((2,)),
             dma((line, GROUPS)),
             dma((line, GROUPS)),
             dma((line, GROUPS)),

time: 258 us -> 250 us (0.969)
  the two profiles are of different devices: /device:TPU:24 before, /device:TPU:3 now
where the time goes in v2:
time: 250 us; the launch traced here: 249 us
  Pallas kernels  244 us (98%)
  local copies, waits for them, and re-layouts  5.21 us (2%)
    pallas_call x1, Pallas kernels, body(): pl.pallas_call(functools.partial(kernel, n, terms), out_shape=jax.ShapeDt...  244 us
    unnamed x2, local copies, waits for them, and re-layouts  5.21 us

profile of v2, /device:TPU:3, one launch (start us, length us, event | category | flops | bytes accessed | tf_op | source)
XLA Modules:
  0.0 249.5 jit_solution(2317371334218605471)
XLA Ops:
  0.0 1.4 copy.6.sectors
  1.4 244.2 %shard_map.55 = bf16[24,128,512]{2,1,0:T(8,128)(2,1)} custom-call(s32[24,2]{1,0:T(8,128)} %copy.6.sectors, s32[1,24]{1,0:T(1,128)} %sources.1, bf16[24,512,512]{2,1,0:T(8,128)(2,1)} %psi_h.1, bf16[16,64,512]{2,1,0:T(8,128)(2,1)} %bitcast.2, bf16[16,64,512]{2,1,0:T(8,128)(2,1)} %bitcast.3), custom_call_target="tpu_custom_call" | custom-call | flops 12884901888 | bytes 29360128 | tf_op jit(solution)/shard_map/pallas_call | solution.py:349
  245.6 3.9 %copy.8 = bf16[24,128,512]{2,1,0:T(8,128)(2,1)} copy(bf16[24,128,512]{2,1,0:T(8,128)(2,1)} %shard_map.55) | data formatting | bytes 6291456

commit v3 on v2

--- a/solution.py
+++ b/solution.py
@@ -9,6 +9,10 @@
 
 MESH = pl.DeviceIdType.MESH
 GROUPS = 4
+
+
+def halves_of(rows):
+    return 2 if rows % 32 == 0 else 1
 
 
 def kernel(
@@ -42,8 +46,11 @@
     tiles = psi_h.shape[0]
     rows = right_h.shape[1]
     line = n // 2
-    wide = 2 * rows
-    per_owner = line // terms
+    halves = halves_of(rows)
+    part = rows // halves
+    wide = 2 * part
+    units = line * halves
+    per_owner = units // terms
     size = tiles // GROUPS
     term = lax.axis_index("term")
     sec = lax.axis_index("sec")
@@ -57,14 +64,16 @@
     has_up = spot + 1 < line
     has_down = spot > 0
     mate = spot + 1 - 2 * lax.rem(spot, 2)
-    gathered = (right_v, left_v)
-    owned = (right_h, left_h)
+    kinds = range(1, 1 + halves)
+    owned = [right_h] + [left_h.at[:, pl.ds(h * part, part), :] for h in range(halves)]
 
     def slot_of(place, parity):
         return place * 2 + parity
 
     def window(kind, slot):
-        return gathered[kind].at[:, pl.ds(pl.multiple_of(slot * rows, rows), rows), :]
+        if kind == 0:
+            return right_v.at[:, pl.ds(pl.multiple_of(slot * rows, rows), rows), :]
+        return left_v.at[:, pl.ds(pl.multiple_of(slot * rows + (kind - 1) * part, part), part), :]
 
     def env_copy(kind, slot, src, target, sem):
         return pltpu.make_async_remote_copy(
@@ -184,7 +193,9 @@
     locals_ = (
         pltpu.make_async_copy(psi_h, psi_v, local_sem.at[0]),
         pltpu.make_async_copy(right_h, window(0, sec), local_sem.at[1]),
-        pltpu.make_async_copy(left_h, window(1, sec), local_sem.at[2]),
+        pltpu.make_async_copy(
+            left_h, left_v.at[:, pl.ds(pl.multiple_of(sec * rows, rows), rows), :], local_sem.at[2]
+        ),
     )
     for copy in locals_:
         copy.start()
@@ -209,19 +220,22 @@
         chosen = right_v[sectors[k, 1]]
         half_v[k] = jnp.dot(moved, chosen, preferred_element_type=jnp.float32).astype(jnp.bfloat16)
 
-    def apply_left(block):
+    def apply_left(place, kind):
+        block = place * halves + kind - 1
         owner = block // per_owner
         owner_core = lax.rem(owner, 2)
         owner_chip = owner // 2
-        await_slot(1, slot_of(block, 1 - side))
-
-        @pl.when(block == spot)
-        def _():
-            to_mate(1).start()
+        await_slot(kind, slot_of(place, 1 - side))
+
+        @pl.when(place == spot)
+        def _():
+            to_mate(kind).start()
 
         @pl.loop(0, left_v.shape[0])
         def _(i):
-            left_now[i] = left_v[i, block_rows(block), :]
+            for parity in range(2):
+                start = pl.multiple_of((place * 2 + parity) * rows + (kind - 1) * part, part)
+                left_now[i, parity * part : (parity + 1) * part] = left_v[i, pl.ds(start, part), :]
 
         @pl.loop(0, GROUPS)
         def _(group):
@@ -256,26 +270,37 @@
 
                 chip_copy(block, group).start()
 
-    @pl.loop(0, line)
-    def _(step):
-        @pl.when(step > 1)
-        def _():
-            forward(1, step)
-
-        @pl.when(spot - step >= 0)
-        def _():
-            apply_left(spot - step)
-
-        @pl.when((step > 0) & (spot + step < line))
-        def _():
-            apply_left(spot + step)
-
-    def out_copy(j, group):
-        block = term * per_owner + j
+    for kind in kinds:
+        if kind > 1:
+            forward(kind, 1)
+
+        @pl.loop(0, line)
+        def _(step):
+            @pl.when(step > 1)
+            def _():
+                forward(kind, step)
+
+            if kind < halves:
+
+                @pl.when(step == line - 2)
+                def _():
+                    push_own(kind + 1)
+
+            @pl.when(spot - step >= 0)
+            def _():
+                apply_left(spot - step, kind)
+
+            @pl.when((step > 0) & (spot + step < line))
+            def _():
+                apply_left(spot + step, kind)
+
+    def out_copy(j, group, parity):
+        start = (term * per_owner + j) * wide + parity * part
+        target = (j // halves) * 2 * rows + parity * rows + lax.rem(j, halves) * part
         return pltpu.make_async_copy(
-            psi_v.at[group_rows(group), block_rows(block), :],
-            out_h.at[group_rows(group), pl.ds(pl.multiple_of(j * wide, wide), wide), :],
-            out_sem.at[j, group],
+            psi_v.at[group_rows(group), pl.ds(pl.multiple_of(start, part), part), :],
+            out_h.at[group_rows(group), pl.ds(pl.multiple_of(target, part), part), :],
+            out_sem.at[j, group, parity],
         )
 
     @pl.loop(0, per_owner)
@@ -296,9 +321,11 @@
                     + chip_in[j, k].astype(jnp.float32)
                 ).astype(jnp.bfloat16)
 
-            out_copy(j, group).start()
-
-    to_mate(1).wait_send()
+            for parity in range(2):
+                out_copy(j, group, parity).start()
+
+    for kind in kinds:
+        to_mate(kind).wait_send()
 
     @pl.loop(0, line)
     def _(place):
@@ -306,9 +333,10 @@
 
         @pl.when(place != mate)
         def _():
-            to_pair(1, place, owned[1]).wait_send()
-
-        for kind in range(2):
+            for kind in kinds:
+                to_pair(kind, place, owned[kind]).wait_send()
+
+        for kind in range(1 + halves):
 
             @pl.when(has_up & (place <= spot))
             def _():
@@ -318,6 +346,8 @@
             def _():
                 to_down(kind, place, owned[kind]).wait_send()
 
+    @pl.loop(0, units)
+    def _(place):
         owner = place // per_owner
 
         @pl.loop(0, GROUPS)
@@ -334,7 +364,8 @@
     def _(j):
         @pl.loop(0, GROUPS)
         def _(group):
-            out_copy(j, group).wait()
+            for parity in range(2):
+                out_copy(j, group, parity).wait()
 
 
 def body(psi_tiles, sectors, sources, left_env, right_env):
@@ -343,7 +374,9 @@
     tiles, width, _ = psi_tiles.shape
     nsec = left_env.shape[1]
     line = n // 2
-    wide = 2 * width // n
+    halves = halves_of(width // n)
+    wide = 2 * width // n // halves
+    units = line * halves
     kind = jnp.bfloat16
     dma = pltpu.SemaphoreType.DMA
     return pl.pallas_call(
@@ -357,19 +390,19 @@
             pltpu.VMEM((nsec, width, width), kind),
             pltpu.VMEM((nsec, wide, width), kind),
             pltpu.VMEM((tiles, width, width), kind),
-            pltpu.VMEM((line // 2, tiles, wide, width), kind),
-            pltpu.VMEM((line // terms, tiles, wide, width), kind),
+            pltpu.VMEM((units // 2, tiles, wide, width), kind),
+            pltpu.VMEM((units // terms, tiles, wide, width), kind),
             dma((3,)),
-            dma((2, n)),
-            dma((2, line)),
-            dma((2, line)),
-            dma((2, line)),
-            dma((2,)),
-            dma((line, GROUPS)),
-            dma((line, GROUPS)),
-            dma((line, GROUPS)),
-            dma((line, GROUPS)),
-            dma((line // terms, GROUPS)),
+            dma((1 + halves, n)),
+            dma((1 + halves, line)),
+            dma((1 + halves, line)),
+            dma((1 + halves, line)),
+            dma((1 + halves,)),
+            dma((units, GROUPS)),
+            dma((units, GROUPS)),
+            dma((units, GROUPS)),
+            dma((units, GROUPS)),
+            dma((units // terms, GROUPS, 2)),
         ],
         compiler_params=pltpu.CompilerParams(
             collective_id=0, has_side_effects=True, vmem_limit_bytes=60 * 1024 * 1024

time: 250 us -> 236 us (0.944)
  the two profiles are of different devices: /device:TPU:3 before, /device:TPU:24 now
where the time goes in v3:
time: 236 us
  Pallas kernels  231 us (98%)
  local copies, waits for them, and re-layouts  5.21 us (2%)
    pallas_call x1, Pallas kernels, body(): pl.pallas_call(functools.partial(kernel, n, terms), out_shape=jax.ShapeDt...  231 us
    unnamed x2, local copies, waits for them, and re-layouts  5.21 us

profile of v3, /device:TPU:24, one launch (start us, length us, event | category | flops | bytes accessed | tf_op | source)
XLA Modules:
  0.0 236.2 jit_solution(13166135051120250806)
XLA Ops:
  0.0 1.4 copy.6.sectors
  1.4 231.0 %shard_map.55 = bf16[24,128,512]{2,1,0:T(8,128)(2,1)} custom-call(s32[24,2]{1,0:T(8,128)} %copy.6.sectors, s32[1,24]{1,0:T(1,128)} %sources.1, bf16[24,512,512]{2,1,0:T(8,128)(2,1)} %psi_h.1, bf16[16,64,512]{2,1,0:T(8,128)(2,1)} %bitcast.2, bf16[16,64,512]{2,1,0:T(8,128)(2,1)} %bitcast.3), custom_call_target="tpu_custom_call" | custom-call | flops 12884901888 | bytes 29360128 | tf_op jit(solution)/shard_map/pallas_call | solution.py:382
  232.3 3.9 %copy.8 = bf16[24,128,512]{2,1,0:T(8,128)(2,1)} copy(bf16[24,128,512]{2,1,0:T(8,128)(2,1)} %shard_map.55) | data formatting | bytes 6291456
